TPU v7x, 512 devices: a whole 4x8x8 slice. The times are simulated.
512 devices in a mesh: gx: 16 (over z, core), gy: 32 (over x, y).
Axes of the slice: x: 4, y: 8, z: 8, core: 2. Of those that a mesh axis runs over, the one named last changes fastest.
Arguments:
- points_in: bfloat16 [16, 1048576], P(None, ('gx', 'gy')), may hold values from -6 to 6
- near_blocks: bfloat16 [16384, 64, 256], P(('gx', 'gy')), may hold values from -0.375 to 0.375
- near_source: int32 [16384, 4], P(('gx', 'gy')), may hold values from 0 to 16383, as said below
- near_count: int32 [16384], P(('gx', 'gy')), may hold values from 1 to 4
- col_basis: bfloat16 [64, 1048576], P(None, ('gx', 'gy')), may hold values from -0.75 to 0.75
- row_basis: bfloat16 [64, 1048576], P(None, ('gx', 'gy')), may hold values from -0.75 to 0.75
- up_transfer: bfloat16 [16384, 64, 64], P(('gx', 'gy')), may hold values from -0.125 to 0.125
- down_transfer: bfloat16 [16384, 64, 64], P(('gx', 'gy')), may hold values from -0.75 to 0.75
- leaf_rank: int32 [16384], P(('gx', 'gy')), may hold values from 32 to 64
- kind_table: bfloat16 [16, 64, 64], replicated, may hold values from -0.375 to 0.375
- far_source: int32 [16384, 4], P(('gx', 'gy')), may hold values from 0 to 16383, as said below
- far_kind: int32 [16384, 4], P(('gx', 'gy')), may hold values from 0 to 15
- root_rank: int32 [512], P(('gx', 'gy')), may hold values from 32 to 64
- root_coupling: bfloat16 [512, 8, 64, 64], P(('gx', 'gy')), may hold values from -0.25 to 0.25
- root_source: int32 [512, 8], P(('gx', 'gy')), may hold values from 0 to 31, as said below
- plane_up: bfloat16 [512, 64, 64], P(('gx', 'gy')), may hold values from -0.75 to 0.75
- plane_down: bfloat16 [512, 64, 64], P(('gx', 'gy')), may hold values from -0.75 to 0.75
- plane_coupling: bfloat16 [16, 16, 64, 64], P('gx'), may hold values from -0.03125 to 0.03125
Outputs:
- product: bfloat16 [16, 1048576], P(None, ('gx', 'gy'))
Inputs may be any that keep to these rules, and one draw needn't show every extreme that they name: `near_source`: slot 0 of each leaf is the leaf itself; every other slot names a leaf of the same root, or one of the last 16 leaves of the root with the next lower gy index, or one of the first 16 leaves of the root with the next higher gy index (same gx index). `far_source`: each source is a leaf of the root with the same gy index and a gx index one lower or one higher. `root_source`: A root's sources differ from its own gy index, and from the two next to it, modulo 32.
All inputs are finite; a program needn't handle non-finite values.
Results may differ from a plain program's by a relative error of at most 0.007.
Values may be sent and summed in bfloat16 or wider, within the bound.
A program may use at most 64 MiB of HBM per device.

v0:
```python
import jax
import jax.numpy as jnp
from jax import lax
from jax.sharding import PartitionSpec as P

BORDER = 16


highest = lax.Precision.HIGHEST


def with_halo(cells, sides, width):
    for axis, dim in sides:
        count = lax.axis_size(axis)
        ends = count - 1
        head = lax.slice_in_dim(cells, 0, width, axis=dim)
        tail = lax.slice_in_dim(cells, cells.shape[dim] - width, cells.shape[dim], axis=dim)
        cells = jnp.concatenate(
            [
                lax.ppermute(tail, axis, [(i, (i + 1) % count) for i in range(ends)]),
                cells,
                lax.ppermute(head, axis, [((i + 1) % count, i) for i in range(ends)]),
            ],
            axis=dim,
        )
    return cells


def per_device(
    points_in,
    near_blocks,
    near_source,
    near_count,
    col_basis,
    row_basis,
    up_transfer,
    down_transfer,
    leaf_rank,
    kind_table,
    far_source,
    far_kind,
    root_rank,
    root_coupling,
    root_source,
    plane_up,
    plane_down,
    plane_coupling,
):
    rhs_count, local_points = points_in.shape
    leaf_count = leaf_rank.shape[0]
    leaf_size = local_points // leaf_count
    rank_max = col_basis.shape[0]
    near_width = near_source.shape[1]
    far_width = far_source.shape[1]
    kind_count = kind_table.shape[0]
    planes = lax.axis_size("gx")
    plane_roots = lax.axis_size("gy")
    plane_index = lax.axis_index("gx")
    row_index = lax.axis_index("gy")
    device = plane_index * plane_roots + row_index
    first_leaf = device * leaf_count
    padded = with_halo(points_in, (("gy", 1),), BORDER * leaf_size)
    stacked = padded.reshape(rhs_count, leaf_count + 2 * BORDER, leaf_size)
    local_source = near_source - first_leaf + BORDER
    picked = jnp.take(stacked, local_source.reshape(-1), axis=1).reshape(
        rhs_count, leaf_count, near_width, leaf_size
    )
    live_slots = lax.broadcasted_iota(jnp.int32, near_source.shape, 1) < near_count[:, None]
    picked = jnp.where(live_slots[None, :, :, None], picked, jnp.zeros((), jnp.bfloat16))
    near_part = jnp.einsum(
        "rlm,lpm->rlp",
        picked.reshape(rhs_count, leaf_count, near_width * leaf_size),
        near_blocks,
        preferred_element_type=jnp.float32,
    )
    rank_iota = lax.broadcasted_iota(jnp.int32, (1, rank_max), 1)
    keep_leaf = rank_iota < leaf_rank[:, None]
    col_rows = col_basis.reshape(rank_max, leaf_count, leaf_size)
    coeffs = jnp.einsum(
        "klp,rlp->lkr",
        col_rows,
        points_in.reshape(rhs_count, leaf_count, leaf_size),
        preferred_element_type=jnp.float32,
    )
    coeffs = jnp.where(keep_leaf[:, :, None], coeffs, 0.0).astype(jnp.bfloat16)
    flat_coeffs = coeffs.reshape(1, leaf_count, rank_max * rhs_count)
    beside_all = with_halo(flat_coeffs, (("gx", 0),), 1).reshape(
        3 * leaf_count, rank_max * rhs_count
    )
    source_device = far_source // leaf_count
    far_slot = (
        source_device // plane_roots - plane_index + 1
    ) * leaf_count + far_source % leaf_count
    sources = jnp.take(beside_all, far_slot.reshape(-1), axis=0).reshape(
        leaf_count, far_width, rank_max, rhs_count
    )
    onehot = (
        far_kind[:, :, None] == lax.broadcasted_iota(jnp.int32, (1, 1, kind_count), 2)
    ).astype(jnp.bfloat16)
    matrices = jnp.einsum(
        "lct,tm->lcm",
        onehot,
        kind_table.reshape(kind_count, rank_max * rank_max),
        preferred_element_type=jnp.float32,
    )
    matrices = matrices.astype(jnp.bfloat16).reshape(leaf_count, far_width, rank_max, rank_max)
    leaf_out = jnp.einsum("lcjk,lckr->ljr", matrices, sources, preferred_element_type=jnp.float32)
    keep_root = rank_iota[0] < root_rank[0]
    root_coeffs = jnp.einsum("lkj,lkr->jr", up_transfer, coeffs, preferred_element_type=jnp.float32)
    root_coeffs = jnp.where(keep_root[:, None], root_coeffs, 0.0).astype(jnp.bfloat16)
    partial_value = jnp.einsum(
        "ji,jr->ir",
        plane_up[0].astype(jnp.float32),
        root_coeffs.astype(jnp.float32),
        precision=highest,
    )
    every_root, every_part = (
        lax.all_gather(root_coeffs.astype(jnp.float32)[None], ("gx", "gy"), axis=0, tiled=True),
        lax.all_gather(partial_value[None], ("gx", "gy"), axis=0, tiled=True),
    )
    row_coeffs = lax.dynamic_slice_in_dim(
        every_root, plane_index * plane_roots, plane_roots, 0
    ).astype(jnp.bfloat16)
    plane_values = every_part.reshape(planes, plane_roots, rank_max, rhs_count).sum(axis=1)
    chooser = (
        root_source[0][:, None] == lax.broadcasted_iota(jnp.int32, (1, plane_roots), 1)
    ).astype(jnp.bfloat16)
    chosen = jnp.einsum(
        "cs,skr->ckr", chooser, row_coeffs, preferred_element_type=jnp.float32
    ).astype(jnp.bfloat16)
    root_out = jnp.einsum(
        "cjk,ckr->jr", root_coupling[0], chosen, preferred_element_type=jnp.float32
    )
    plane_ids = lax.broadcasted_iota(jnp.int32, (planes,), 0)
    far_mask = (jnp.abs(plane_ids - plane_index) >= 2).astype(jnp.float32)
    plane_out = jnp.einsum(
        "qij,q,qjr->ir",
        plane_coupling[0].astype(jnp.float32),
        far_mask,
        plane_values,
        precision=highest,
    )
    root_out = root_out + jnp.einsum(
        "ji,ir->jr", plane_down[0].astype(jnp.float32), plane_out, precision=highest
    )
    root_out = jnp.where(keep_root[:, None], root_out, 0.0).astype(jnp.bfloat16)
    leaf_out = leaf_out + jnp.einsum(
        "lkj,jr->lkr", down_transfer, root_out, preferred_element_type=jnp.float32
    )
    leaf_out = jnp.where(keep_leaf[:, :, None], leaf_out, 0.0).astype(jnp.bfloat16)
    far_part = jnp.einsum(
        "klp,lkr->rlp",
        row_basis.reshape(rank_max, leaf_count, leaf_size),
        leaf_out,
        preferred_element_type=jnp.float32,
    )
    return (near_part + far_part).reshape(rhs_count, local_points).astype(jnp.bfloat16)


def solution(mesh):
    return jax.shard_map(
        per_device,
        mesh=mesh,
        in_specs=(
            P(None, ("gx", "gy")),
            P(("gx", "gy"), None, None),
            P(("gx", "gy"), None),
            P(("gx", "gy")),
            P(None, ("gx", "gy")),
            P(None, ("gx", "gy")),
            P(("gx", "gy"), None, None),
            P(("gx", "gy"), None, None),
            P(("gx", "gy")),
            P(),
            P(("gx", "gy"), None),
            P(("gx", "gy"), None),
            P(("gx", "gy")),
            P(("gx", "gy"), None, None, None),
            P(("gx", "gy"), None),
            P(("gx", "gy"), None, None),
            P(("gx", "gy"), None, None),
            P("gx", None, None, None),
        ),
        out_specs=P(None, ("gx", "gy")),
        check_vma=False,
    )
```

profile of v0, /device:TPU:1, one launch (start us, length us, event | category | flops | bytes accessed | tf_op | source)
XLA Modules:
  0.0 264.9 jit_solution(14642181666128071929)
XLA Ops:
  6.6 1.6 reshape.165
  8.2 1.0 reshape.166
  9.2 0.7 iota_compare_fusion.2
  11.0 1.9 fusion.13
  13.0 1.4 convolution_bitcast_fusion.1
  14.7 8.8 %collective-permute-start.3 = (bf16[1,32,1024]{1,2,0:T(8,128)(2,1)S(1)}, bf16[1,32,1024]{1,2,0:T(8,128)(2,1)S(1)}, u32[]{:S(2)}, u32[]{:S(2)}) collective-permute-start(bf16[1,32,1024]{1,2,0:T(8,128)(2,1)S(1)} %bitcast.75), channel_id=1, source_target_pairs={{32,0},{64,32},{96,64},{128,96},{160,128},{192,160},{224,192},{256... | collective-permute-start | bytes 196616 | tf_op jit(solution)/shard_map/ppermute | solution.py:22
  23.5 1.9 collective-permute-start.2
  25.4 1.3 collective-permute-start.1
  26.7 4.0 %collective-permute-start = (bf16[16,1024]{1,0:T(8,128)(2,1)S(1)}, bf16[16,1024]{1,0:T(8,128)(2,1)S(1)}, u32[]{:S(2)}, u32[]{:S(2)}) collective-permute-start(bf16[16,1024]{1,0:T(8,128)(2,1)S(1)} %get-tuple-element.7), channel_id=1, source_target_pairs={{0,1},{1,2},{2,3},{3,4},{4,5},{5,6},{6,7},{7,8},{8,9},{9,10},{10,1... | collective-permute-start | bytes 98312 | tf_op jit(solution)/shard_map/ppermute | solution.py:20
  31.6 0.5 convolution_convert_fusion
  32.1 0.5 compare_convert_fusion
  33.3 3.4 %reshape.164 = bf16[32,4,64,64]{3,2,0,1:T(8,128)(2,1)} reshape(bf16[32,4,4096]{2,0,1:T(8,128)(2,1)S(1)} %convolution_convert_fusion) | data formatting | bytes 2097152 | tf_op jit(solution)/shard_map/reshape | solution.py:106
  36.8 1.3 reshape.171
  38.6 0.7 gather_fusion
  39.8 1.1 fusion.19
  41.2 1.6 gather_fusion.1
  42.8 3.4 %gather.15 = bf16[32,4,64,16]{3,2,1,0:T(8,128)(2,1)} reshape(bf16[128,1024]{1,0:T(8,128)(2,1)} %gather_fusion.1) | data formatting | bytes 524288 | tf_op jit(solution)/shard_map/jit(_take)/gather | solution.py:94
  46.2 3.0 %fusion.4 = f32[32,64,16]{1,2,0:T(8,128)S(1)} fusion(bf16[32,4,64,64]{3,2,0,1:T(8,128)(2,1)S(1)} %copy-done.1, bf16[32,4,64,16]{3,2,1,0:T(8,128)(2,1)} %gather.15, pred[32,4]{1,0:T(8,128)(4,1)S(1)} %copy.59), kind=kOutput, calls=%fused_computation.12 | convolution fusion | flops 16908288 | bytes 1441920 | tf_op jit(solution)/shard_map/lcjk,lckr->ljr/dot_general | solution.py:107
  49.2 85.1 %all-gather.7.cloned.1.call-done = bf16[512,64,16]{1,2,0:T(8,128)(2,1)} async-done(((bf16[1,64,16]{1,2,0:T(8,128)(2,1)}), bf16[512,64,16]{1,2,0:T(8,128)(2,1)}) %all-gather.7.cloned.1.call-update) | async-done | bytes 1048592 | tf_op jit(solution)/shard_map/all_gather | solution.py:118
  134.3 0.9 constant_dynamic-slice_fusion
  135.6 117.8 %all-gather.9.cloned.1.call-done = f32[512,64,16]{1,2,0:T(8,128)} async-done(((f32[1,64,16]{1,2,0:T(8,128)}), f32[512,64,16]{1,2,0:T(8,128)}) %all-gather.9.cloned.1.call-update) | async-done | bytes 2097168 | tf_op jit(solution)/shard_map/all_gather | solution.py:119
  253.4 2.5 bitcast_reduce_fusion
  256.5 0.7 fusion.10
  257.2 0.8 convert_element_type.53
  (82 shorter events, 4.5 us)
Async XLA Ops:
  6.5 33.3 %copy-start = (bf16[32,64,256]{2,1,0:T(8,128)(2,1)S(1)}, bf16[32,64,256]{2,1,0:T(8,128)(2,1)}, u32[]{:S(2)}) copy-start(bf16[32,64,256]{2,1,0:T(8,128)(2,1)} %param.19) | copy-start | bytes 3145732
  6.5 18.9 %copy-start.4 = (bf16[16,2048]{1,0:T(8,128)(2,1)S(1)}, bf16[16,2048]{1,0:T(8,128)(2,1)}, u32[]{:S(2)}) copy-start(bf16[16,2048]{1,0:T(8,128)(2,1)} %param.18) | copy-start | bytes 196612
  6.5 6.4 %copy-start.10 = (bf16[1,64,64]{2,1,0:T(8,128)(2,1)S(1)}, bf16[1,64,64]{2,1,0:T(8,128)(2,1)}, u32[]{:S(2)}) copy-start(bf16[1,64,64]{2,1,0:T(8,128)(2,1)} %param.33) | copy-start | bytes 24580
  6.5 24.2 %copy-start.12 = (s32[32,4]{0,1:T(4,128)S(1)}, s32[32,4]{0,1:T(4,128)}, u32[]{:S(2)}) copy-start(s32[32,4]{0,1:T(4,128)} %param.20) | copy-start | bytes 1540
  6.5 24.4 %copy-start.8 = (bf16[16,64,64]{2,1,0:T(8,128)(2,1)S(1)}, bf16[16,64,64]{2,1,0:T(8,128)(2,1)}, u32[]{:S(2)}) copy-start(bf16[16,64,64]{2,1,0:T(8,128)(2,1)} %param.27) | copy-start | bytes 393220
  6.5 24.7 %copy-start.14 = (s32[32,4]{0,1:T(4,128)S(1)}, s32[32,4]{0,1:T(4,128)}, u32[]{:S(2)}) copy-start(s32[32,4]{0,1:T(4,128)} %param.28) | copy-start | bytes 1540
  6.6 25.0 %copy-start.17 = (s32[32]{0:T(128)S(1)}, s32[32]{0:T(128)}, u32[]{:S(2)}) copy-start(s32[32]{0:T(128)} %param.21) | copy-start | bytes 388
  6.6 25.1 %copy-start.13 = (s32[32,4]{0,1:T(4,128)S(1)}, s32[32,4]{0,1:T(4,128)}, u32[]{:S(2)}) copy-start(s32[32,4]{0,1:T(4,128)} %param.29) | copy-start | bytes 1540
  6.6 127.7 %all-gather.7.cloned.1.call-start = ((), (), s32[]{:S(2)}) async-start(), calls=%async_computation | async-start | bytes 2101248 | tf_op jit(solution)/shard_map/all_gather | solution.py:118
  12.9 240.5 %all-gather.9.cloned.1.call-start = ((), (), s32[]{:S(2)}) async-start(), calls=%async_computation.1 | async-start | bytes 4202496 | tf_op jit(solution)/shard_map/all_gather | solution.py:119
  14.7 26.2 %collective-permute-start.3 = (bf16[1,32,1024]{1,2,0:T(8,128)(2,1)S(1)}, bf16[1,32,1024]{1,2,0:T(8,128)(2,1)S(1)}, u32[]{:S(2)}, u32[]{:S(2)}) collective-permute-start(bf16[1,32,1024]{1,2,0:T(8,128)(2,1)S(1)} %bitcast.75), channel_id=1, source_target_pairs={{32,0},{64,32},{96,64},{128,96},{160,128},{192,160},{224,192},{256... | collective-permute-start | bytes 196616 | tf_op jit(solution)/shard_map/ppermute | solution.py:22
  23.5 17.5 %collective-permute-start.2 = (bf16[1,32,1024]{1,2,0:T(8,128)(2,1)S(1)}, bf16[1,32,1024]{1,2,0:T(8,128)(2,1)S(1)}, u32[]{:S(2)}, u32[]{:S(2)}) collective-permute-start(bf16[1,32,1024]{1,2,0:T(8,128)(2,1)S(1)} %bitcast.76), channel_id=1, source_target_pairs={{0,32},{32,64},{64,96},{96,128},{128,160},{160,192},{192,224},{224... | collective-permute-start | bytes 196616 | tf_op jit(solution)/shard_map/ppermute | solution.py:20
  25.4 12.7 %collective-permute-start.1 = (bf16[16,1024]{1,0:T(8,128)(2,1)S(1)}, bf16[16,1024]{1,0:T(8,128)(2,1)S(1)}, u32[]{:S(2)}, u32[]{:S(2)}) collective-permute-start(bf16[16,1024]{1,0:T(8,128)(2,1)S(1)} %get-tuple-element.8), channel_id=1, source_target_pairs={{1,0},{2,1},{3,2},{4,3},{5,4},{6,5},{7,6},{8,7},{9,8},{10,9},{11,1... | collective-permute-start | bytes 98312 | tf_op jit(solution)/shard_map/ppermute | solution.py:22
  26.7 11.4 %collective-permute-start = (bf16[16,1024]{1,0:T(8,128)(2,1)S(1)}, bf16[16,1024]{1,0:T(8,128)(2,1)S(1)}, u32[]{:S(2)}, u32[]{:S(2)}) collective-permute-start(bf16[16,1024]{1,0:T(8,128)(2,1)S(1)} %get-tuple-element.7), channel_id=1, source_target_pairs={{0,1},{1,2},{2,3},{3,4},{4,5},{5,6},{6,7},{7,8},{8,9},{9,10},{10,1... | collective-permute-start | bytes 98312 | tf_op jit(solution)/shard_map/ppermute | solution.py:20
  31.6 5.1 %copy-start.6 = (bf16[64,2048]{1,0:T(8,128)(2,1)S(1)}, bf16[64,2048]{1,0:T(8,128)(2,1)}, u32[]{:S(2)}) copy-start(bf16[64,2048]{1,0:T(8,128)(2,1)} %param.23) | copy-start | bytes 786436
  41.2 5.0 %copy-start.1 = (bf16[32,4,64,64]{3,2,0,1:T(8,128)(2,1)S(1)}, bf16[32,4,64,64]{3,2,0,1:T(8,128)(2,1)}, u32[]{:S(2)}) copy-start(bf16[32,4,64,64]{3,2,0,1:T(8,128)(2,1)} %reshape.164) | copy-start | bytes 3145732
  46.2 89.0 %copy-start.15 = (s32[1,8]{1,0:T(1,128)S(1)}, s32[1,8]{1,0:T(1,128)}, u32[]{:S(2)}) copy-start(s32[1,8]{1,0:T(1,128)} %param.32) | copy-start | bytes 100
  46.2 89.2 %copy-start.9 = (bf16[1,8,64,64]{3,2,1,0:T(8,128)(2,1)S(1)}, bf16[1,8,64,64]{3,2,1,0:T(8,128)(2,1)}, u32[]{:S(2)}) copy-start(bf16[1,8,64,64]{3,2,1,0:T(8,128)(2,1)} %param.31) | copy-start | bytes 196612
  135.5 120.4 %copy-start.7 = (bf16[1,16,64,64]{3,2,1,0:T(8,128)(2,1)S(1)}, bf16[1,16,64,64]{3,2,1,0:T(8,128)(2,1)}, u32[]{:S(2)}) copy-start(bf16[1,16,64,64]{3,2,1,0:T(8,128)(2,1)} %param.35) | copy-start | bytes 393220
  135.5 120.4 %copy-start.16 = (f32[16]{0:T(128)S(1)}, f32[16]{0:T(128)}, u32[]{:S(2)}) copy-start(f32[16]{0:T(128)} %compare_convert_fusion) | copy-start | bytes 196
  135.5 120.8 %copy-start.11 = (bf16[1,64,64]{2,1,0:T(8,128)(2,1)S(1)}, bf16[1,64,64]{2,1,0:T(8,128)(2,1)}, u32[]{:S(2)}) copy-start(bf16[1,64,64]{2,1,0:T(8,128)(2,1)} %param.34) | copy-start | bytes 24580
  135.6 120.9 %copy-start.2 = (bf16[64,32,64]{2,1,0:T(8,128)(2,1)S(1)}, bf16[64,32,64]{2,1,0:T(8,128)(2,1)}, u32[]{:S(2)}) copy-start(bf16[64,32,64]{2,1,0:T(8,128)(2,1)} %reshape.171) | copy-start | bytes 786436
  135.6 120.9 %copy-start.3 = (f32[32,16,64]{2,1,0:T(8,128)S(1)}, f32[32,16,64]{2,1,0:T(8,128)}, u32[]{:S(2)}) copy-start(f32[32,16,64]{2,1,0:T(8,128)} %fusion.19) | copy-start | bytes 393220
  135.6 120.9 %copy-start.5 = (bf16[32,64,64]{2,1,0:T(8,128)(2,1)S(1)}, bf16[32,64,64]{2,1,0:T(8,128)(2,1)}, u32[]{:S(2)}) copy-start(bf16[32,64,64]{2,1,0:T(8,128)(2,1)} %param.25) | copy-start | bytes 786436
Sparse Core Ops, SparseCore 0:
  13.0 121.1 all-gather.6
  138.5 114.9 all-gather.8
where the time goes:
time: 265 us
  waiting for transfers between devices  203 us (77%)
  local copies, waits for them, and re-layouts  17.6 us (7%)
  starting transfers between devices  16.1 us (6%)
  between operations  14.5 us (5%)
  matrix products  9.75 us (4%)
  other arithmetic  3.97 us (1%)
    all_gather x1, waiting for transfers between devices, per_device(): lax.all_gather(partial_value[None], ('gx', 'gy'), axis=0, tiled=True)  118 us
    all_gather x1, waiting for transfers between devices, per_device(): lax.all_gather(root_coeffs.astype(jnp.float32)[None], ('gx', 'gy'), axis=...  85.1 us
    ppermute x2, starting transfers between devices, with_halo(): lax.ppermute(head, axis, [((i + 1) % count, i) for i in range(ends)])  10.1 us
    ppermute x2, starting transfers between devices, with_halo(): lax.ppermute(tail, axis, [(i, (i + 1) % count) for i in range(ends)])  5.91 us
  transfers between devices with their start and end apart: 6, of which 2 were waited for; matrix products, arithmetic and copies ran while one was open for 8% of the time, Pallas kernels for 0%

commit v1 on v0

v1 whole, which is shorter than its diff:
```python
import jax
import jax.numpy as jnp
from jax import lax
from jax.experimental import pallas as pl
from jax.experimental.pallas import tpu as pltpu
from jax.sharding import PartitionSpec as P

MESH = pl.DeviceIdType.MESH
BF = jnp.bfloat16
F32 = jnp.float32

RHS = 16
LEAVES = 32
RANK = 64
BORDER = 16
GX = 16
GY = 32
NEAR = 4
FAR = 4
KINDS = 16
ROOT_SLOTS = 8
CHUNKS = 8
SPAN = LEAVES * RANK


def dot_nt(a, b):
    return lax.dot_general(a, b, (((1,), (1,)), ((), ())), preferred_element_type=F32)


def dot_nn(a, b):
    return lax.dot_general(a, b, (((1,), (0,)), ((), ())), preferred_element_type=F32)


def kernel(
    points,
    col,
    up,
    plane_up,
    plane_coupling,
    near_blocks,
    kind_table,
    row,
    root_coupling,
    down,
    plane_down,
    near_source,
    near_count,
    leaf_rank,
    far_source,
    far_kind,
    root_rank,
    root_source,
    out,
    points_v,
    col_v,
    up_v,
    pu_v,
    pc_v,
    near_v,
    kind_v,
    row_v,
    rc_v,
    down_v,
    pd_v,
    points_halo,
    coef,
    coef_halo,
    part_buf,
    root_buf,
    sum_buf,
    near_left,
    near_right,
    far_left,
    far_right,
    kind_left,
    kind_right,
    pc_cat,
    rc_cat,
    row_diag,
    keep_lanes,
    far_rows,
    near_rows,
    load_sem,
    halo_send,
    halo_recv,
    gather_send,
    gather_recv,
):
    gx = lax.axis_index("gx")
    gy = lax.axis_index("gy")
    first_leaf = (gx * GY + gy) * LEAVES

    loads = []
    for place, (src, dst) in enumerate(
        (
            (points, points_v),
            (col, col_v),
            (up, up_v),
            (plane_up.at[0], pu_v),
            (plane_coupling.at[0], pc_v),
            (near_blocks, near_v),
            (kind_table, kind_v),
            (row, row_v),
            (root_coupling.at[0], rc_v),
            (down, down_v),
            (plane_down.at[0], pd_v),
        )
    ):
        loads.append(pltpu.make_async_copy(src, dst, load_sem.at[place]))
        loads[-1].start()
    (
        load_points,
        load_col,
        load_up,
        load_pu,
        load_pc,
        load_near,
        load_kind,
        load_row,
        load_rc,
        load_down,
        load_pd,
    ) = loads

    barrier = pltpu.get_barrier_semaphore()

    def greet_gx(i, carry):
        pl.semaphore_signal(
            barrier, inc=1, device_id=(lax.rem(gx + i, GX), gy), device_id_type=MESH
        )
        return carry

    def greet_gy(i, carry):
        pl.semaphore_signal(
            barrier, inc=1, device_id=(gx, lax.rem(gy + i, GY)), device_id_type=MESH
        )
        return carry

    lax.fori_loop(1, GX, greet_gx, 0)
    lax.fori_loop(1, GY, greet_gy, 0)

    lane = lax.broadcasted_iota(jnp.int32, (RHS, 128), 1)
    low = lane < RANK
    left_mask = low.astype(F32).astype(BF)
    right_mask = (lane >= RANK).astype(F32).astype(BF)
    lane_leaf = lax.broadcasted_iota(jnp.int32, (RANK, 256), 1) // RANK
    leaf_masks = [(lane_leaf == i).astype(F32).astype(BF) for i in range(4)]

    def block_diag(block):
        return jnp.concatenate([block * mask for mask in leaf_masks], axis=0)

    def diagonal(full):
        first = jnp.where(low, full[0:16, 0:128], full[16:32, 0:128])
        second = jnp.where(low, full[32:48, 128:256], full[48:64, 128:256])
        return jnp.concatenate([first, second], axis=1)

    lane_rank = lax.broadcasted_iota(jnp.int32, (8, 128), 1)
    in_low = lane_rank < RANK
    rank_of_lane = jnp.where(in_low, lane_rank, lane_rank - RANK)
    for pair in range(LEAVES // 2):
        ranks = jnp.where(in_low, leaf_rank[2 * pair], leaf_rank[2 * pair + 1])
        keep_lanes[:, 128 * pair : 128 * pair + 128] = (rank_of_lane < ranks).astype(F32)

    load_points.wait()
    load_col.wait()
    for c in range(CHUNKS):
        span = slice(256 * c, 256 * c + 256)
        full = dot_nt(points_v[:, span], block_diag(col_v[:, span]))
        keep = jnp.concatenate([keep_lanes[:, span]] * 2, axis=0)
        coef[:, span] = jnp.where(keep > 0.0, full, 0.0).astype(BF)

    load_up.wait()
    root = jnp.zeros((RHS, RANK), F32)
    for c in range(CHUNKS):
        root = root + dot_nn(
            coef[:, 256 * c : 256 * c + 256], up_v[4 * c : 4 * c + 4].reshape(256, RANK)
        )
    root_keep = lax.broadcasted_iota(jnp.int32, (RHS, RANK), 1) < root_rank[0]
    root = jnp.where(root_keep, root, 0.0)
    load_pu.wait()
    part = dot_nn(root.astype(BF), pu_v[...])
    part_buf[gx] = jnp.concatenate([part, part], axis=1).astype(BF)
    root_buf[gy] = jnp.concatenate([root, root], axis=1).astype(BF)

    pl.semaphore_wait(barrier, GX - 1 + GY - 1)

    def spread_gx(buf, place):
        def send(i, carry):
            pltpu.make_async_remote_copy(
                src_ref=buf.at[gx],
                dst_ref=buf.at[gx],
                send_sem=gather_send.at[place],
                recv_sem=gather_recv.at[place],
                device_id=(lax.rem(gx + i, GX), gy),
                device_id_type=MESH,
            ).start()
            return carry

        lax.fori_loop(1, GX, send, 0)

    def spread_gy(buf, place):
        def send(i, carry):
            pltpu.make_async_remote_copy(
                src_ref=buf.at[gy],
                dst_ref=buf.at[gy],
                send_sem=gather_send.at[place],
                recv_sem=gather_recv.at[place],
                device_id=(gx, lax.rem(gy + i, GY)),
                device_id_type=MESH,
            ).start()
            return carry

        lax.fori_loop(1, GY, send, 0)

    def wait_all(sem, buf, count):
        held = buf.at[pl.ds(0, count)]
        pltpu.make_async_copy(held, held, sem).wait()

    spread_gx(part_buf, 0)
    next_gx = (lax.rem(gx + 1, GX), gy)
    last_gx = (lax.rem(gx + GX - 1, GX), gy)
    next_gy = (gx, lax.rem(gy + 1, GY))
    last_gy = (gx, lax.rem(gy + GY - 1, GY))
    half = BORDER * RANK
    halos = []
    for place, (src, dst, device) in enumerate(
        (
            (points_v.at[:, pl.ds(half, half)], points_halo.at[0], next_gy),
            (points_v.at[:, pl.ds(0, half)], points_halo.at[1], last_gy),
            (coef, coef_halo.at[0], next_gx),
            (coef, coef_halo.at[1], last_gx),
        )
    ):
        halos.append(
            pltpu.make_async_remote_copy(
                src_ref=src,
                dst_ref=dst,
                send_sem=halo_send.at[place],
                recv_sem=halo_recv.at[place],
                device_id=device,
                device_id_type=MESH,
            )
        )
        halos[-1].start()
    spread_gy(root_buf, 1)

    load_pc.wait()
    for pair in range(GX // 2):
        blocks = []
        for q in (2 * pair, 2 * pair + 1):
            far = (jnp.abs(gx - q) >= 2).astype(F32).astype(BF)
            blocks.append(pc_v[q] * far)
        pc_cat[:, 128 * pair : 128 * pair + 128] = jnp.concatenate(blocks, axis=1)
    load_kind.wait()
    zero_block = jnp.zeros((RANK, RANK), BF)
    for t in range(KINDS):
        kind_left[t] = jnp.concatenate([kind_v[t], zero_block], axis=1)
        kind_right[t] = jnp.concatenate([zero_block, kind_v[t]], axis=1)
    load_rc.wait()
    for pair in range(ROOT_SLOTS // 2):
        rc_cat[:, 128 * pair : 128 * pair + 128] = jnp.concatenate(
            [rc_v[2 * pair], rc_v[2 * pair + 1]], axis=1
        )

    def expand(x, left, right, place):
        turned = jnp.concatenate([x[:, RANK:], x[:, :RANK]], axis=1)
        left[place] = x * left_mask
        right[place + 1] = x * right_mask
        left[place + 1] = turned * left_mask
        right[place] = turned * right_mask

    for pair in range(LEAVES // 2):
        expand(points_v[:, 128 * pair : 128 * pair + 128], near_left, near_right, BORDER + 2 * pair)
    window = 2 * LEAVES
    near_left[window] = jnp.zeros((RHS, 128), BF)
    near_right[window] = jnp.zeros((RHS, 128), BF)

    wait_all(gather_recv.at[0], part_buf, GX - 1)
    lhs = [
        part_buf[2 * pair] * left_mask + part_buf[2 * pair + 1] * right_mask
        for pair in range(GX // 2)
    ]
    plane = dot_nt(jnp.concatenate(lhs, axis=1), pc_cat[...])
    high = plane.astype(BF).astype(F32)
    sum_buf[gy] = jnp.concatenate([high, plane - high], axis=1).astype(BF)
    spread_gy(sum_buf, 2)

    halos[0].wait_recv()
    halos[1].wait_recv()
    for side in range(2):
        for pair in range(BORDER // 2):
            expand(
                points_halo[side, :, 128 * pair : 128 * pair + 128],
                near_left,
                near_right,
                side * (BORDER + LEAVES) + 2 * pair,
            )
    load_near.wait()
    for c in range(CHUNKS):
        rows = []
        for leaf in range(4 * c, 4 * c + 4):
            count = near_count[leaf]
            places = []
            for slot in range(NEAR):
                place = near_source[slot, leaf] - first_leaf + BORDER
                place = jnp.minimum(jnp.maximum(place, 0), window - 1)
                places.append(jnp.where(slot < count, place, window))
            rows.append(
                jnp.concatenate(
                    [
                        near_left[places[0]] + near_right[places[1]],
                        near_left[places[2]] + near_right[places[3]],
                    ],
                    axis=1,
                )
            )
        full = dot_nt(jnp.concatenate(rows, axis=0), near_v[4 * c : 4 * c + 4].reshape(256, 256))
        near_rows[:, 256 * c : 256 * c + 256] = diagonal(full)

    load_row.wait()
    for c in range(CHUNKS):
        row_diag[c] = block_diag(row_v[:, 256 * c : 256 * c + 256])

    halos[2].wait_recv()
    halos[3].wait_recv()
    for side in range(2):
        for pair in range(LEAVES // 2):
            expand(
                coef_halo[side, :, 128 * pair : 128 * pair + 128],
                far_left,
                far_right,
                side * LEAVES + 2 * pair,
            )
    for c in range(CHUNKS):
        rows = []
        matrices = []
        for leaf in range(4 * c, 4 * c + 4):
            places = []
            kinds = []
            for slot in range(FAR):
                source = far_source[slot, leaf] - first_leaf
                place = jnp.where(
                    source < 0, source + GY * LEAVES, source - GY * LEAVES + LEAVES
                )
                places.append(jnp.minimum(jnp.maximum(place, 0), window - 1))
                kinds.append(far_kind[slot, leaf])
            rows.append(
                jnp.concatenate(
                    [
                        far_left[places[0]] + far_right[places[1]],
                        far_left[places[2]] + far_right[places[3]],
                    ],
                    axis=1,
                )
            )
            matrices.append(
                jnp.concatenate(
                    [
                        kind_left[kinds[0]] + kind_right[kinds[1]],
                        kind_left[kinds[2]] + kind_right[kinds[3]],
                    ],
                    axis=1,
                )
            )
        full = dot_nt(jnp.concatenate(rows, axis=0), jnp.concatenate(matrices, axis=0))
        far_rows[:, 256 * c : 256 * c + 256] = diagonal(full)

    wait_all(gather_recv.at[1], root_buf, GY - 1)
    chosen = [
        root_buf[root_source[0, 2 * pair]] * left_mask
        + root_buf[root_source[0, 2 * pair + 1]] * right_mask
        for pair in range(ROOT_SLOTS // 2)
    ]
    beside = dot_nt(jnp.concatenate(chosen, axis=1), rc_cat[...])
    load_down.wait()
    load_pd.wait()

    wait_all(gather_recv.at[2], sum_buf, GY - 1)
    total = [sum_buf[q].astype(F32) for q in range(GY)]
    while len(total) > 1:
        total = [a + b for a, b in zip(total[0::2], total[1::2])]
    plane_out = total[0][:, :RANK] + total[0][:, RANK:]
    root_out = beside + dot_nt(plane_out.astype(BF), pd_v[...])
    root_out = jnp.where(root_keep, root_out, 0.0).astype(BF)
    for c in range(CHUNKS):
        span = slice(256 * c, 256 * c + 256)
        leaf_out = far_rows[:, span] + dot_nt(
            root_out, down_v[4 * c : 4 * c + 4].reshape(256, RANK)
        )
        keep = jnp.concatenate([keep_lanes[:, span]] * 2, axis=0)
        leaf_out = jnp.where(keep > 0.0, leaf_out, 0.0).astype(BF)
        out[:, span] = (near_rows[:, span] + dot_nn(leaf_out, row_diag[c])).astype(BF)

    for halo in halos:
        halo.wait_send()
    wait_all(gather_send.at[0], part_buf, GX - 1)
    wait_all(gather_send.at[1], root_buf, GY - 1)
    wait_all(gather_send.at[2], sum_buf, GY - 1)


def per_device(
    points_in,
    near_blocks,
    near_source,
    near_count,
    col_basis,
    row_basis,
    up_transfer,
    down_transfer,
    leaf_rank,
    kind_table,
    far_source,
    far_kind,
    root_rank,
    root_coupling,
    root_source,
    plane_up,
    plane_down,
    plane_coupling,
):
    hbm = pl.BlockSpec(memory_space=pl.ANY)
    smem = pl.BlockSpec(memory_space=pltpu.SMEM)
    return pl.pallas_call(
        kernel,
        out_shape=jax.ShapeDtypeStruct((RHS, SPAN), BF),
        in_specs=[hbm] * 11 + [smem] * 7,
        out_specs=pl.BlockSpec(memory_space=pltpu.VMEM),
        scratch_shapes=[
            pltpu.VMEM((RHS, SPAN), BF),
            pltpu.VMEM((RANK, SPAN), BF),
            pltpu.VMEM((LEAVES, RANK, RANK), BF),
            pltpu.VMEM((RANK, RANK), BF),
            pltpu.VMEM((GX, RANK, RANK), BF),
            pltpu.VMEM((LEAVES, RANK, NEAR * RANK), BF),
            pltpu.VMEM((KINDS, RANK, RANK), BF),
            pltpu.VMEM((RANK, SPAN), BF),
            pltpu.VMEM((ROOT_SLOTS, RANK, RANK), BF),
            pltpu.VMEM((LEAVES, RANK, RANK), BF),
            pltpu.VMEM((RANK, RANK), BF),
            pltpu.VMEM((2, RHS, BORDER * RANK), BF),
            pltpu.VMEM((RHS, SPAN), BF),
            pltpu.VMEM((2, RHS, SPAN), BF),
            pltpu.VMEM((GX, RHS, 128), BF),
            pltpu.VMEM((GY, RHS, 128), BF),
            pltpu.VMEM((GY, RHS, 128), BF),
            pltpu.VMEM((2 * LEAVES + 1, RHS, 128), BF),
            pltpu.VMEM((2 * LEAVES + 1, RHS, 128), BF),
            pltpu.VMEM((2 * LEAVES, RHS, 128), BF),
            pltpu.VMEM((2 * LEAVES, RHS, 128), BF),
            pltpu.VMEM((KINDS, RANK, 128), BF),
            pltpu.VMEM((KINDS, RANK, 128), BF),
            pltpu.VMEM((RANK, GX * RANK), BF),
            pltpu.VMEM((RANK, ROOT_SLOTS * RANK), BF),
            pltpu.VMEM((CHUNKS, 256, 256), BF),
            pltpu.VMEM((8, SPAN), F32),
            pltpu.VMEM((RHS, SPAN), F32),
            pltpu.VMEM((RHS, SPAN), F32),
            pltpu.SemaphoreType.DMA((11,)),
            pltpu.SemaphoreType.DMA((4,)),
            pltpu.SemaphoreType.DMA((4,)),
            pltpu.SemaphoreType.DMA((3,)),
            pltpu.SemaphoreType.DMA((3,)),
        ],
        compiler_params=pltpu.CompilerParams(
            collective_id=0, has_side_effects=True, vmem_limit_bytes=32 * 2**20
        ),
        name="h2_product",
    )(
        points_in,
        col_basis,
        up_transfer,
        plane_up,
        plane_coupling,
        near_blocks,
        kind_table,
        row_basis,
        root_coupling,
        down_transfer,
        plane_down,
        near_source.T,
        near_count,
        leaf_rank,
        far_source.T,
        far_kind.T,
        root_rank,
        root_source,
    )


def solution(mesh):
    return jax.shard_map(
        per_device,
        mesh=mesh,
        in_specs=(
            P(None, ("gx", "gy")),
            P(("gx", "gy"), None, None),
            P(("gx", "gy"), None),
            P(("gx", "gy")),
            P(None, ("gx", "gy")),
            P(None, ("gx", "gy")),
            P(("gx", "gy"), None, None),
            P(("gx", "gy"), None, None),
            P(("gx", "gy")),
            P(),
            P(("gx", "gy"), None),
            P(("gx", "gy"), None),
            P(("gx", "gy")),
            P(("gx", "gy"), None, None, None),
            P(("gx", "gy"), None),
            P(("gx", "gy"), None, None),
            P(("gx", "gy"), None, None),
            P("gx", None, None, None),
        ),
        out_specs=P(None, ("gx", "gy")),
        check_vma=False,
    )
```

time: 265 us -> 41.4 us (0.16)
  waiting for transfers between devices: 203 us -> 0 us
  Pallas kernels: 0 us -> 28.5 us
  starting transfers between devices: 16.1 us -> 0 us
  between operations: 14.5 us -> 0.74 us
  matrix products: 9.75 us -> 0 us
  local copies, waits for them, and re-layouts: 17.6 us -> 11.6 us
  other arithmetic: 3.97 us -> 0 us
    all_gather x2 -> x0, waiting for transfers between devices: 203 us -> none  [the longest x1 118 us: per_device(): lax.all_gather(partial_value[None], ('gx', 'gy'), axis=0, tiled=True)]
    pallas_call x0 -> x1, Pallas kernels: none -> 28.5 us  [per_device(): pl.pallas_call(kernel, out_shape=jax.ShapeDtypeStruct((RHS, SPAN), BF), i...]
    ppermute x4 -> x0, starting transfers between devices: 16 us -> none  [the longest x2 10.1 us: with_halo(): lax.ppermute(head, axis, [((i + 1) % count, i) for i in range(ends)])]
    unnamed x36 -> x35, local copies, waits for them, and re-layouts: 0.11 us -> 11.6 us
    dot_general x11 -> x0, matrix products: 9.75 us -> none  [the longest x1 3 us: per_device(): jnp.einsum('lcjk,lckr->ljr', matrices, sources, preferred_element_type=jn...]
    reshape x10 -> x0, local copies, waits for them, and re-layouts: 8.29 us -> none  [the longest x1 3.36 us: per_device(): matrices.astype(jnp.bfloat16)]
    gather x5 -> x0, local copies, waits for them, and re-layouts: 6.16 us -> none  [the longest x2 4.99 us: per_device(): jnp.take(beside_all, far_slot.reshape(-1), axis=0)]
  transfers between devices with their start and end apart: 6 -> 0, of which waited for: 2 -> 0; matrix products, arithmetic and copies ran while one was open for 8% -> 0% of each run, Pallas kernels for 0% -> 0%
where the time goes in v1:
time: 41.4 us; the launch traced here: 40.8 us
  Pallas kernels  28.5 us (69%)
  local copies, waits for them, and re-layouts  11.6 us (28%)
  between operations  0.74 us (2%)
    pallas_call x1, Pallas kernels, per_device(): pl.pallas_call(kernel, out_shape=jax.ShapeDtypeStruct((RHS, SPAN), BF), i...  28.5 us
    unnamed x35, local copies, waits for them, and re-layouts  11.6 us

profile of v1, /device:TPU:1, one launch (start us, length us, event | category | flops | bytes accessed | tf_op | source)
XLA Modules:
  0.0 40.8 jit_solution(4452430824265841758)
XLA Ops:
  0.7 0.0 copy-start.12
  0.7 0.0 copy-start.11
  0.7 0.0 copy-start.14
  0.7 0.0 copy-start.15
  0.7 0.0 copy-start.16
  0.7 0.0 copy-done.13
  0.7 0.6 %copy-done.12 = s32[32,4]{0,1:T(4,128)S(1)} copy-done((s32[32,4]{0,1:T(4,128)S(1)}, s32[32,4]{0,1:T(4,128)}, u32[]{:S(2)}) %copy-start.12) | copy-done | bytes 536
  1.4 0.0 copy-done.11
  1.4 0.0 copy-done.14
  1.4 0.0 copy-done.15
  1.4 0.0 copy-done.16
  1.4 1.2 %copy-done = bf16[32,64,256]{2,1,0:T(8,128)(2,1)S(1)} copy-done((bf16[32,64,256]{2,1,0:T(8,128)(2,1)S(1)}, bf16[32,64,256]{2,1,0:T(8,128)(2,1)}, u32[]{:S(2)}) %copy-start) | copy-done | bytes 1048600
  2.6 1.0 %copy-done.1 = bf16[32,64,64]{2,1,0:T(8,128)(2,1)S(1)} copy-done((bf16[32,64,64]{2,1,0:T(8,128)(2,1)S(1)}, bf16[32,64,64]{2,1,0:T(8,128)(2,1)}, u32[]{:S(2)}) %copy-start.1) | copy-done | bytes 262168
  3.7 1.0 %copy-done.2 = bf16[32,64,64]{2,1,0:T(8,128)(2,1)S(1)} copy-done((bf16[32,64,64]{2,1,0:T(8,128)(2,1)S(1)}, bf16[32,64,64]{2,1,0:T(8,128)(2,1)}, u32[]{:S(2)}) %copy-start.2) | copy-done | bytes 262168
  4.7 0.9 %copy-done.3 = bf16[64,2048]{1,0:T(8,128)(2,1)S(1)} copy-done((bf16[64,2048]{1,0:T(8,128)(2,1)S(1)}, bf16[64,2048]{1,0:T(8,128)(2,1)}, u32[]{:S(2)}) %copy-start.3) | copy-done | bytes 262168
  5.7 0.9 %copy-done.4 = bf16[1,16,64,64]{3,2,1,0:T(8,128)(2,1)S(1)} copy-done((bf16[1,16,64,64]{3,2,1,0:T(8,128)(2,1)S(1)}, bf16[1,16,64,64]{3,2,1,0:T(8,128)(2,1)}, u32[]{:S(2)}) %copy-start.4) | copy-done | bytes 131096
  6.6 0.9 %copy-done.5 = bf16[16,64,64]{2,1,0:T(8,128)(2,1)S(1)} copy-done((bf16[16,64,64]{2,1,0:T(8,128)(2,1)S(1)}, bf16[16,64,64]{2,1,0:T(8,128)(2,1)}, u32[]{:S(2)}) %copy-start.5) | copy-done | bytes 131096
  7.6 0.9 %copy-done.6 = bf16[64,2048]{1,0:T(8,128)(2,1)S(1)} copy-done((bf16[64,2048]{1,0:T(8,128)(2,1)S(1)}, bf16[64,2048]{1,0:T(8,128)(2,1)}, u32[]{:S(2)}) %copy-start.6) | copy-done | bytes 262168
  8.5 0.9 %copy-done.7 = bf16[1,8,64,64]{3,2,1,0:T(8,128)(2,1)S(1)} copy-done((bf16[1,8,64,64]{3,2,1,0:T(8,128)(2,1)S(1)}, bf16[1,8,64,64]{3,2,1,0:T(8,128)(2,1)}, u32[]{:S(2)}) %copy-start.7) | copy-done | bytes 65560
  9.4 0.8 %copy-done.8 = bf16[16,2048]{1,0:T(8,128)(2,1)S(1)} copy-done((bf16[16,2048]{1,0:T(8,128)(2,1)S(1)}, bf16[16,2048]{1,0:T(8,128)(2,1)}, u32[]{:S(2)}) %copy-start.8) | copy-done | bytes 65560
  10.2 0.7 %copy-done.9 = bf16[1,64,64]{2,1,0:T(8,128)(2,1)S(1)} copy-done((bf16[1,64,64]{2,1,0:T(8,128)(2,1)S(1)}, bf16[1,64,64]{2,1,0:T(8,128)(2,1)}, u32[]{:S(2)}) %copy-start.9) | copy-done | bytes 8216
  11.0 0.7 %copy-done.10 = bf16[1,64,64]{2,1,0:T(8,128)(2,1)S(1)} copy-done((bf16[1,64,64]{2,1,0:T(8,128)(2,1)S(1)}, bf16[1,64,64]{2,1,0:T(8,128)(2,1)}, u32[]{:S(2)}) %copy-start.10) | copy-done | bytes 8216
  11.7 28.5 %h2_product.1 = bf16[16,2048]{1,0:T(8,128)(2,1)S(1)} custom-call(bf16[16,2048]{1,0:T(8,128)(2,1)S(1)} %copy-done.8, bf16[64,2048]{1,0:T(8,128)(2,1)S(1)} %copy-done.3, bf16[32,64,64]{2,1,0:T(8,128)(2,1)S(1)} %copy-done.1, bf16[1,64,64]{2,1,0:T(8,128)(2,1)S(1)} %copy-done.9, bf16[1,16,64,64]{3,2,1,0:T(8,128)(2,1)S(1)} %copy-done.4, ...), custom_call_target="tpu_custom_call" | custom-call | tf_op jit(solution)/shard_map/h2_product/pallas_call | solution.py:423
  40.2 0.6 %copy.21 = bf16[16,2048]{1,0:T(8,128)(2,1)} copy(bf16[16,2048]{1,0:T(8,128)(2,1)S(1)} %h2_product.1) | data formatting | bytes 131072
  (12 shorter events, 0.0 us)
Async XLA Ops:
  0.0 0.7 %copy-start.13 = (s32[32,4]{0,1:T(4,128)S(1)}, s32[32,4]{0,1:T(4,128)}, u32[]{:S(2)}) copy-start(s32[32,4]{0,1:T(4,128)} %param.29) | copy-start | bytes 1540
  0.7 0.7 %copy-start.12 = (s32[32,4]{0,1:T(4,128)S(1)}, s32[32,4]{0,1:T(4,128)}, u32[]{:S(2)}) copy-start(s32[32,4]{0,1:T(4,128)} %param.28) | copy-start | bytes 1540
  0.7 0.7 %copy-start.11 = (s32[32,4]{0,1:T(4,128)S(1)}, s32[32,4]{0,1:T(4,128)}, u32[]{:S(2)}) copy-start(s32[32,4]{0,1:T(4,128)} %param.20) | copy-start | bytes 1540
  0.7 0.7 %copy-start.14 = (s32[32]{0:T(128)S(1)}, s32[32]{0:T(128)}, u32[]{:S(2)}) copy-start(s32[32]{0:T(128)} %near_count.1) | copy-start | bytes 388
  0.7 0.7 %copy-start.15 = (s32[32]{0:T(128)S(1)}, s32[32]{0:T(128)}, u32[]{:S(2)}) copy-start(s32[32]{0:T(128)} %leaf_rank.1) | copy-start | bytes 388
  0.7 0.7 %copy-start.16 = (s32[1,8]{1,0:T(1,128)S(1)}, s32[1,8]{1,0:T(1,128)}, u32[]{:S(2)}) copy-start(s32[1,8]{1,0:T(1,128)} %root_source.1) | copy-start | bytes 100
  1.4 1.2 %copy-start = (bf16[32,64,256]{2,1,0:T(8,128)(2,1)S(1)}, bf16[32,64,256]{2,1,0:T(8,128)(2,1)}, u32[]{:S(2)}) copy-start(bf16[32,64,256]{2,1,0:T(8,128)(2,1)} %near_blocks.1) | copy-start | bytes 3145732
  2.6 1.0 %copy-start.1 = (bf16[32,64,64]{2,1,0:T(8,128)(2,1)S(1)}, bf16[32,64,64]{2,1,0:T(8,128)(2,1)}, u32[]{:S(2)}) copy-start(bf16[32,64,64]{2,1,0:T(8,128)(2,1)} %up.1) | copy-start | bytes 786436
  3.7 1.0 %copy-start.2 = (bf16[32,64,64]{2,1,0:T(8,128)(2,1)S(1)}, bf16[32,64,64]{2,1,0:T(8,128)(2,1)}, u32[]{:S(2)}) copy-start(bf16[32,64,64]{2,1,0:T(8,128)(2,1)} %down.1) | copy-start | bytes 786436
  4.7 0.9 %copy-start.3 = (bf16[64,2048]{1,0:T(8,128)(2,1)S(1)}, bf16[64,2048]{1,0:T(8,128)(2,1)}, u32[]{:S(2)}) copy-start(bf16[64,2048]{1,0:T(8,128)(2,1)} %col.1) | copy-start | bytes 786436
  5.6 0.9 %copy-start.4 = (bf16[1,16,64,64]{3,2,1,0:T(8,128)(2,1)S(1)}, bf16[1,16,64,64]{3,2,1,0:T(8,128)(2,1)}, u32[]{:S(2)}) copy-start(bf16[1,16,64,64]{3,2,1,0:T(8,128)(2,1)} %plane_coupling.1) | copy-start | bytes 393220
  6.6 0.9 %copy-start.5 = (bf16[16,64,64]{2,1,0:T(8,128)(2,1)S(1)}, bf16[16,64,64]{2,1,0:T(8,128)(2,1)}, u32[]{:S(2)}) copy-start(bf16[16,64,64]{2,1,0:T(8,128)(2,1)} %kind_table.1) | copy-start | bytes 393220
  7.5 0.9 %copy-start.6 = (bf16[64,2048]{1,0:T(8,128)(2,1)S(1)}, bf16[64,2048]{1,0:T(8,128)(2,1)}, u32[]{:S(2)}) copy-start(bf16[64,2048]{1,0:T(8,128)(2,1)} %row.1) | copy-start | bytes 786436
  8.5 0.9 %copy-start.7 = (bf16[1,8,64,64]{3,2,1,0:T(8,128)(2,1)S(1)}, bf16[1,8,64,64]{3,2,1,0:T(8,128)(2,1)}, u32[]{:S(2)}) copy-start(bf16[1,8,64,64]{3,2,1,0:T(8,128)(2,1)} %root_coupling.1) | copy-start | bytes 196612
  9.4 0.8 %copy-start.8 = (bf16[16,2048]{1,0:T(8,128)(2,1)S(1)}, bf16[16,2048]{1,0:T(8,128)(2,1)}, u32[]{:S(2)}) copy-start(bf16[16,2048]{1,0:T(8,128)(2,1)} %points.1) | copy-start | bytes 196612
  10.2 0.7 %copy-start.9 = (bf16[1,64,64]{2,1,0:T(8,128)(2,1)S(1)}, bf16[1,64,64]{2,1,0:T(8,128)(2,1)}, u32[]{:S(2)}) copy-start(bf16[1,64,64]{2,1,0:T(8,128)(2,1)} %plane_up.1) | copy-start | bytes 24580
  11.0 0.7 %copy-start.10 = (bf16[1,64,64]{2,1,0:T(8,128)(2,1)S(1)}, bf16[1,64,64]{2,1,0:T(8,128)(2,1)}, u32[]{:S(2)}) copy-start(bf16[1,64,64]{2,1,0:T(8,128)(2,1)} %plane_down.1) | copy-start | bytes 24580

commit v2 on v1

--- a/solution.py
+++ b/solution.py
@@ -43,14 +43,20 @@
     root_coupling,
     down,
     plane_down,
+    near_source_h,
+    near_count_h,
+    leaf_rank_h,
+    far_source_h,
+    far_kind_h,
+    root_rank,
+    root_source_h,
+    out,
     near_source,
     near_count,
     leaf_rank,
     far_source,
     far_kind,
-    root_rank,
     root_source,
-    out,
     points_v,
     col_v,
     up_v,
@@ -76,7 +82,7 @@
     kind_right,
     pc_cat,
     rc_cat,
-    row_diag,
+    plane_map,
     keep_lanes,
     far_rows,
     near_rows,
@@ -90,37 +96,50 @@
     gy = lax.axis_index("gy")
     first_leaf = (gx * GY + gy) * LEAVES
 
-    loads = []
-    for place, (src, dst) in enumerate(
-        (
-            (points, points_v),
-            (col, col_v),
-            (up, up_v),
-            (plane_up.at[0], pu_v),
-            (plane_coupling.at[0], pc_v),
-            (near_blocks, near_v),
-            (kind_table, kind_v),
-            (row, row_v),
-            (root_coupling.at[0], rc_v),
-            (down, down_v),
-            (plane_down.at[0], pd_v),
-        )
-    ):
-        loads.append(pltpu.make_async_copy(src, dst, load_sem.at[place]))
-        loads[-1].start()
+    pairs = (
+        (leaf_rank_h, leaf_rank),
+        (points, points_v),
+        (col, col_v),
+        (up, up_v),
+        (plane_up.at[0], pu_v),
+        (plane_coupling.at[0], pc_v),
+        (near_source_h, near_source),
+        (near_count_h, near_count),
+        (near_blocks, near_v),
+        (kind_table, kind_v),
+        (row, row_v),
+        (root_coupling.at[0], rc_v),
+        (down, down_v),
+        (plane_down.at[0], pd_v),
+        (far_source_h, far_source),
+        (far_kind_h, far_kind),
+        (root_source_h, root_source),
+    )
+    loads = [
+        pltpu.make_async_copy(src, dst, load_sem.at[place])
+        for place, (src, dst) in enumerate(pairs)
+    ]
     (
+        load_leaf_rank,
         load_points,
         load_col,
         load_up,
         load_pu,
         load_pc,
+        load_near_source,
+        load_near_count,
         load_near,
         load_kind,
         load_row,
         load_rc,
         load_down,
         load_pd,
+        load_far_source,
+        load_far_kind,
+        load_root_source,
     ) = loads
+    for load in loads[:5]:
+        load.start()
 
     barrier = pltpu.get_barrier_semaphore()
 
@@ -157,6 +176,7 @@
     lane_rank = lax.broadcasted_iota(jnp.int32, (8, 128), 1)
     in_low = lane_rank < RANK
     rank_of_lane = jnp.where(in_low, lane_rank, lane_rank - RANK)
+    load_leaf_rank.wait()
     for pair in range(LEAVES // 2):
         ranks = jnp.where(in_low, leaf_rank[2 * pair], leaf_rank[2 * pair + 1])
         keep_lanes[:, 128 * pair : 128 * pair + 128] = (rank_of_lane < ranks).astype(F32)
@@ -170,6 +190,9 @@
         coef[:, span] = jnp.where(keep > 0.0, full, 0.0).astype(BF)
 
     load_up.wait()
+    load_pu.wait()
+    for load in loads[5:]:
+        load.start()
     root = jnp.zeros((RHS, RANK), F32)
     for c in range(CHUNKS):
         root = root + dot_nn(
@@ -177,7 +200,6 @@
         )
     root_keep = lax.broadcasted_iota(jnp.int32, (RHS, RANK), 1) < root_rank[0]
     root = jnp.where(root_keep, root, 0.0)
-    load_pu.wait()
     part = dot_nn(root.astype(BF), pu_v[...])
     part_buf[gx] = jnp.concatenate([part, part], axis=1).astype(BF)
     root_buf[gy] = jnp.concatenate([root, root], axis=1).astype(BF)
@@ -296,6 +318,8 @@
                 side * (BORDER + LEAVES) + 2 * pair,
             )
     load_near.wait()
+    load_near_source.wait()
+    load_near_count.wait()
     for c in range(CHUNKS):
         rows = []
         for leaf in range(4 * c, 4 * c + 4):
@@ -317,10 +341,6 @@
         full = dot_nt(jnp.concatenate(rows, axis=0), near_v[4 * c : 4 * c + 4].reshape(256, 256))
         near_rows[:, 256 * c : 256 * c + 256] = diagonal(full)
 
-    load_row.wait()
-    for c in range(CHUNKS):
-        row_diag[c] = block_diag(row_v[:, 256 * c : 256 * c + 256])
-
     halos[2].wait_recv()
     halos[3].wait_recv()
     for side in range(2):
@@ -331,6 +351,8 @@
                 far_right,
                 side * LEAVES + 2 * pair,
             )
+    load_far_source.wait()
+    load_far_kind.wait()
     for c in range(CHUNKS):
         rows = []
         matrices = []
@@ -366,30 +388,46 @@
         far_rows[:, 256 * c : 256 * c + 256] = diagonal(full)
 
     wait_all(gather_recv.at[1], root_buf, GY - 1)
+    load_root_source.wait()
     chosen = [
         root_buf[root_source[0, 2 * pair]] * left_mask
         + root_buf[root_source[0, 2 * pair + 1]] * right_mask
         for pair in range(ROOT_SLOTS // 2)
     ]
     beside = dot_nt(jnp.concatenate(chosen, axis=1), rc_cat[...])
+    beside = jnp.where(root_keep, beside, 0.0).astype(BF)
+
+    load_row.wait()
     load_down.wait()
     load_pd.wait()
+    unit = (
+        lax.broadcasted_iota(jnp.int32, (RANK, RANK), 0)
+        == lax.broadcasted_iota(jnp.int32, (RANK, RANK), 1)
+    )
+    plane_turned = dot_nt(unit.astype(F32).astype(BF), pd_v[...])
+    keep_root = lax.broadcasted_iota(jnp.int32, (RANK, RANK), 1) < root_rank[0]
+    plane_turned = jnp.where(keep_root, plane_turned, 0.0).astype(BF)
+    downward = jnp.concatenate([beside, plane_turned], axis=0)
+    for c in range(CHUNKS):
+        span = slice(256 * c, 256 * c + 256)
+        leaf_out = dot_nt(downward, down_v[4 * c : 4 * c + 4].reshape(256, RANK))
+        leaf_out = jnp.concatenate(
+            [leaf_out[:RHS] + far_rows[:, span], leaf_out[RHS:]], axis=0
+        )
+        keep = jnp.concatenate([keep_lanes[:, span]] * 10, axis=0)
+        leaf_out = jnp.where(keep > 0.0, leaf_out, 0.0).astype(BF)
+        values = dot_nn(leaf_out, block_diag(row_v[:, span]))
+        near_rows[:, span] += values[:RHS]
+        plane_map[:, span] = values[RHS:].astype(BF)
 
     wait_all(gather_recv.at[2], sum_buf, GY - 1)
     total = [sum_buf[q].astype(F32) for q in range(GY)]
     while len(total) > 1:
         total = [a + b for a, b in zip(total[0::2], total[1::2])]
-    plane_out = total[0][:, :RANK] + total[0][:, RANK:]
-    root_out = beside + dot_nt(plane_out.astype(BF), pd_v[...])
-    root_out = jnp.where(root_keep, root_out, 0.0).astype(BF)
+    plane_out = (total[0][:, :RANK] + total[0][:, RANK:]).astype(BF)
     for c in range(CHUNKS):
         span = slice(256 * c, 256 * c + 256)
-        leaf_out = far_rows[:, span] + dot_nt(
-            root_out, down_v[4 * c : 4 * c + 4].reshape(256, RANK)
-        )
-        keep = jnp.concatenate([keep_lanes[:, span]] * 2, axis=0)
-        leaf_out = jnp.where(keep > 0.0, leaf_out, 0.0).astype(BF)
-        out[:, span] = (near_rows[:, span] + dot_nn(leaf_out, row_diag[c])).astype(BF)
+        out[:, span] = (near_rows[:, span] + dot_nn(plane_out, plane_map[:, span])).astype(BF)
 
     for halo in halos:
         halo.wait_send()
@@ -418,14 +456,19 @@
     plane_down,
     plane_coupling,
 ):
-    hbm = pl.BlockSpec(memory_space=pl.ANY)
-    smem = pl.BlockSpec(memory_space=pltpu.SMEM)
+    hbm = pl.BlockSpec(memory_space=pltpu.HBM)
     return pl.pallas_call(
         kernel,
         out_shape=jax.ShapeDtypeStruct((RHS, SPAN), BF),
-        in_specs=[hbm] * 11 + [smem] * 7,
+        in_specs=[hbm] * 16 + [pl.BlockSpec(memory_space=pltpu.SMEM), hbm],
         out_specs=pl.BlockSpec(memory_space=pltpu.VMEM),
         scratch_shapes=[
+            pltpu.SMEM((NEAR, LEAVES), jnp.int32),
+            pltpu.SMEM((LEAVES,), jnp.int32),
+            pltpu.SMEM((LEAVES,), jnp.int32),
+            pltpu.SMEM((FAR, LEAVES), jnp.int32),
+            pltpu.SMEM((FAR, LEAVES), jnp.int32),
+            pltpu.SMEM((1, ROOT_SLOTS), jnp.int32),
             pltpu.VMEM((RHS, SPAN), BF),
             pltpu.VMEM((RANK, SPAN), BF),
             pltpu.VMEM((LEAVES, RANK, RANK), BF),
@@ -451,11 +494,11 @@
             pltpu.VMEM((KINDS, RANK, 128), BF),
             pltpu.VMEM((RANK, GX * RANK), BF),
             pltpu.VMEM((RANK, ROOT_SLOTS * RANK), BF),
-            pltpu.VMEM((CHUNKS, 256, 256), BF),
+            pltpu.VMEM((RANK, SPAN), BF),
             pltpu.VMEM((8, SPAN), F32),
             pltpu.VMEM((RHS, SPAN), F32),
             pltpu.VMEM((RHS, SPAN), F32),
-            pltpu.SemaphoreType.DMA((11,)),
+            pltpu.SemaphoreType.DMA((17,)),
             pltpu.SemaphoreType.DMA((4,)),
             pltpu.SemaphoreType.DMA((4,)),
             pltpu.SemaphoreType.DMA((3,)),
@@ -466,24 +509,29 @@
         ),
         name="h2_product",
     )(
-        points_in,
-        col_basis,
-        up_transfer,
-        plane_up,
-        plane_coupling,
-        near_blocks,
-        kind_table,
-        row_basis,
-        root_coupling,
-        down_transfer,
-        plane_down,
-        near_source.T,
-        near_count,
-        leaf_rank,
-        far_source.T,
-        far_kind.T,
-        root_rank,
-        root_source,
+        *(
+            array if array.size == 1 else pltpu.with_memory_space_constraint(array, pltpu.HBM)
+            for array in (
+                points_in,
+                col_basis,
+                up_transfer,
+                plane_up,
+                plane_coupling,
+                near_blocks,
+                kind_table,
+                row_basis,
+                root_coupling,
+                down_transfer,
+                plane_down,
+                near_source.T,
+                near_count,
+                leaf_rank,
+                far_source.T,
+                far_kind.T,
+                root_rank,
+                root_source,
+            )
+        )
     )
 
 

time: 41.4 us -> 28.4 us (0.69)
  local copies, waits for them, and re-layouts: 11.6 us -> 0.63 us
  Pallas kernels: 28.5 us -> 27 us
    unnamed x35 -> x1, local copies, waits for them, and re-layouts: 11.6 us -> 0.63 us
    pallas_call x1, Pallas kernels: 28.5 us -> 27 us  [per_device(): pl.pallas_call(kernel, out_shape=jax.ShapeDtypeStruct((RHS, SPAN), BF), i...]
where the time goes in v2:
time: 28.4 us; the launch traced here: 28.3 us
  Pallas kernels  27 us (95%)
  between operations  0.66 us (2%)
  local copies, waits for them, and re-layouts  0.63 us (2%)
    pallas_call x1, Pallas kernels, per_device(): pl.pallas_call(kernel, out_shape=jax.ShapeDtypeStruct((RHS, SPAN), BF), i...  27 us
    unnamed x1, local copies, waits for them, and re-layouts  0.63 us

profile of v2, /device:TPU:1, one launch (start us, length us, event | category | flops | bytes accessed | tf_op | source)
XLA Modules:
  0.0 28.3 jit_solution(14846731362366924518)
XLA Ops:
  0.7 27.0 %h2_product.1 = bf16[16,2048]{1,0:T(8,128)(2,1)S(1)} custom-call(bf16[16,2048]{1,0:T(8,128)(2,1)} %points.1, bf16[64,2048]{1,0:T(8,128)(2,1)} %col.1, bf16[32,64,64]{2,1,0:T(8,128)(2,1)} %up.1, bf16[1,64,64]{2,1,0:T(8,128)(2,1)} %plane_up.1, bf16[1,16,64,64]{3,2,1,0:T(8,128)(2,1)} %plane_coupling.1, bf16[32,64,256]{2,1,0:T(8,128)(2,1)} %near_blocks.1, ...), custom_call_target="tpu_custom_call" | custom-call | tf_op jit(solution)/shard_map/h2_product/pallas_call | solution.py:460
  27.6 0.6 %copy.21 = bf16[16,2048]{1,0:T(8,128)(2,1)} copy(bf16[16,2048]{1,0:T(8,128)(2,1)S(1)} %h2_product.1) | data formatting | bytes 131072

commit v3 on v2

--- a/solution.py
+++ b/solution.py
@@ -145,13 +145,13 @@
 
     def greet_gx(i, carry):
         pl.semaphore_signal(
-            barrier, inc=1, device_id=(lax.rem(gx + i, GX), gy), device_id_type=MESH
+            barrier, inc=1, device_id=((gx + i) & (GX - 1), gy), device_id_type=MESH
         )
         return carry
 
     def greet_gy(i, carry):
         pl.semaphore_signal(
-            barrier, inc=1, device_id=(gx, lax.rem(gy + i, GY)), device_id_type=MESH
+            barrier, inc=1, device_id=(gx, (gy + i) & (GY - 1)), device_id_type=MESH
         )
         return carry
 
@@ -208,41 +208,43 @@
 
     def spread_gx(buf, place):
         def send(i, carry):
+            peer = i + ((i - gx + GX) >> 4)
             pltpu.make_async_remote_copy(
                 src_ref=buf.at[gx],
                 dst_ref=buf.at[gx],
                 send_sem=gather_send.at[place],
                 recv_sem=gather_recv.at[place],
-                device_id=(lax.rem(gx + i, GX), gy),
+                device_id=(peer, gy),
                 device_id_type=MESH,
             ).start()
             return carry
 
-        lax.fori_loop(1, GX, send, 0)
+        lax.fori_loop(0, GX - 1, send, 0)
 
     def spread_gy(buf, place):
         def send(i, carry):
+            peer = i + ((i - gy + GY) >> 5)
             pltpu.make_async_remote_copy(
                 src_ref=buf.at[gy],
                 dst_ref=buf.at[gy],
                 send_sem=gather_send.at[place],
                 recv_sem=gather_recv.at[place],
-                device_id=(gx, lax.rem(gy + i, GY)),
+                device_id=(gx, peer),
                 device_id_type=MESH,
             ).start()
             return carry
 
-        lax.fori_loop(1, GY, send, 0)
+        lax.fori_loop(0, GY - 1, send, 0)
 
     def wait_all(sem, buf, count):
         held = buf.at[pl.ds(0, count)]
         pltpu.make_async_copy(held, held, sem).wait()
 
     spread_gx(part_buf, 0)
-    next_gx = (lax.rem(gx + 1, GX), gy)
-    last_gx = (lax.rem(gx + GX - 1, GX), gy)
-    next_gy = (gx, lax.rem(gy + 1, GY))
-    last_gy = (gx, lax.rem(gy + GY - 1, GY))
+    next_gx = ((gx + 1) & (GX - 1), gy)
+    last_gx = ((gx - 1) & (GX - 1), gy)
+    next_gy = (gx, (gy + 1) & (GY - 1))
+    last_gy = (gx, (gy - 1) & (GY - 1))
     half = BORDER * RANK
     halos = []
     for place, (src, dst, device) in enumerate(

time: 28.4 us -> 27.5 us (0.968)
  Pallas kernels: 27 us -> 26.1 us
    pallas_call x1, Pallas kernels: 27 us -> 26.1 us  [per_device(): pl.pallas_call(kernel, out_shape=jax.ShapeDtypeStruct((RHS, SPAN), BF), i...]
where the time goes in v3:
time: 27.5 us; the launch traced here: 27.4 us
  Pallas kernels  26.1 us (95%)
  between operations  0.66 us (2%)
  local copies, waits for them, and re-layouts  0.63 us (2%)
    pallas_call x1, Pallas kernels, per_device(): pl.pallas_call(kernel, out_shape=jax.ShapeDtypeStruct((RHS, SPAN), BF), i...  26.1 us
    unnamed x1, local copies, waits for them, and re-layouts  0.63 us

profile of v3, /device:TPU:1, one launch (start us, length us, event | category | flops | bytes accessed | tf_op | source)
XLA Modules:
  0.0 27.4 jit_solution(8589160420964219029)
XLA Ops:
  0.7 26.1 %h2_product.1 = bf16[16,2048]{1,0:T(8,128)(2,1)S(1)} custom-call(bf16[16,2048]{1,0:T(8,128)(2,1)} %points.1, bf16[64,2048]{1,0:T(8,128)(2,1)} %col.1, bf16[32,64,64]{2,1,0:T(8,128)(2,1)} %up.1, bf16[1,64,64]{2,1,0:T(8,128)(2,1)} %plane_up.1, bf16[1,16,64,64]{3,2,1,0:T(8,128)(2,1)} %plane_coupling.1, bf16[32,64,256]{2,1,0:T(8,128)(2,1)} %near_blocks.1, ...), custom_call_target="tpu_custom_call" | custom-call | tf_op jit(solution)/shard_map/h2_product/pallas_call | solution.py:462
  26.8 0.6 %copy.21 = bf16[16,2048]{1,0:T(8,128)(2,1)} copy(bf16[16,2048]{1,0:T(8,128)(2,1)S(1)} %h2_product.1) | data formatting | bytes 131072

commit v4 on v3

--- a/solution.py
+++ b/solution.py
@@ -91,6 +91,7 @@
     halo_recv,
     gather_send,
     gather_recv,
+    part_recv,
 ):
     gx = lax.axis_index("gx")
     gy = lax.axis_index("gy")
@@ -145,7 +146,7 @@
 
     def greet_gx(i, carry):
         pl.semaphore_signal(
-            barrier, inc=1, device_id=((gx + i) & (GX - 1), gy), device_id_type=MESH
+            barrier, inc=1, device_id=(i, gy), device_id_type=MESH
         )
         return carry
 
@@ -155,7 +156,7 @@
         )
         return carry
 
-    lax.fori_loop(1, GX, greet_gx, 0)
+    lax.fori_loop(gx + 1, GX, greet_gx, 0)
     lax.fori_loop(1, GY, greet_gy, 0)
 
     lane = lax.broadcasted_iota(jnp.int32, (RHS, 128), 1)
@@ -204,22 +205,37 @@
     part_buf[gx] = jnp.concatenate([part, part], axis=1).astype(BF)
     root_buf[gy] = jnp.concatenate([root, root], axis=1).astype(BF)
 
-    pl.semaphore_wait(barrier, GX - 1 + GY - 1)
-
-    def spread_gx(buf, place):
-        def send(i, carry):
-            peer = i + ((i - gx + GX) >> 4)
-            pltpu.make_async_remote_copy(
-                src_ref=buf.at[gx],
-                dst_ref=buf.at[gx],
-                send_sem=gather_send.at[place],
-                recv_sem=gather_recv.at[place],
-                device_id=(peer, gy),
-                device_id_type=MESH,
-            ).start()
-            return carry
-
-        lax.fori_loop(0, GX - 1, send, 0)
+    pl.semaphore_wait(barrier, gx + GY - 1)
+
+    def send_part(peer, carry):
+        pltpu.make_async_remote_copy(
+            src_ref=part_buf.at[gx],
+            dst_ref=part_buf.at[gx],
+            send_sem=gather_send.at[0],
+            recv_sem=part_recv.at[gx],
+            device_id=(peer, gy),
+            device_id_type=MESH,
+        ).start()
+        return carry
+
+    def wait_part(peer, carry):
+        held = part_buf.at[peer]
+        pltpu.make_async_copy(held, held, part_recv.at[peer]).wait()
+        return carry
+
+    def answer_part(peer, carry):
+        wait_part(peer, carry)
+        return send_part(peer, carry)
+
+    def send_coef(side, device):
+        return pltpu.make_async_remote_copy(
+            src_ref=coef,
+            dst_ref=coef_halo.at[side],
+            send_sem=halo_send.at[2 + side],
+            recv_sem=halo_recv.at[2 + side],
+            device_id=device,
+            device_id_type=MESH,
+        )
 
     def spread_gy(buf, place):
         def send(i, carry):
@@ -240,9 +256,7 @@
         held = buf.at[pl.ds(0, count)]
         pltpu.make_async_copy(held, held, sem).wait()
 
-    spread_gx(part_buf, 0)
-    next_gx = ((gx + 1) & (GX - 1), gy)
-    last_gx = ((gx - 1) & (GX - 1), gy)
+    lax.fori_loop(0, gx, send_part, 0)
     next_gy = (gx, (gy + 1) & (GY - 1))
     last_gy = (gx, (gy - 1) & (GY - 1))
     half = BORDER * RANK
@@ -251,8 +265,6 @@
         (
             (points_v.at[:, pl.ds(half, half)], points_halo.at[0], next_gy),
             (points_v.at[:, pl.ds(0, half)], points_halo.at[1], last_gy),
-            (coef, coef_halo.at[0], next_gx),
-            (coef, coef_halo.at[1], last_gx),
         )
     ):
         halos.append(
@@ -266,6 +278,11 @@
             )
         )
         halos[-1].start()
+
+    @pl.when(gx > 0)
+    def _():
+        send_coef(1, (gx - 1, gy)).start()
+
     spread_gy(root_buf, 1)
 
     load_pc.wait()
@@ -299,7 +316,13 @@
     near_left[window] = jnp.zeros((RHS, 128), BF)
     near_right[window] = jnp.zeros((RHS, 128), BF)
 
-    wait_all(gather_recv.at[0], part_buf, GX - 1)
+    @pl.when(gx < GX - 1)
+    def _():
+        answer_part(gx + 1, 0)
+        send_coef(0, (gx + 1, gy)).start()
+
+    lax.fori_loop(gx + 2, GX, answer_part, 0)
+    lax.fori_loop(0, gx, wait_part, 0)
     lhs = [
         part_buf[2 * pair] * left_mask + part_buf[2 * pair + 1] * right_mask
         for pair in range(GX // 2)
@@ -343,8 +366,22 @@
         full = dot_nt(jnp.concatenate(rows, axis=0), near_v[4 * c : 4 * c + 4].reshape(256, 256))
         near_rows[:, 256 * c : 256 * c + 256] = diagonal(full)
 
-    halos[2].wait_recv()
-    halos[3].wait_recv()
+    @pl.when(gx > 0)
+    def _():
+        send_coef(0, (gx - 1, gy)).wait_recv()
+
+    @pl.when(gx == 0)
+    def _():
+        coef_halo[0] = jnp.zeros((RHS, SPAN), BF)
+
+    @pl.when(gx < GX - 1)
+    def _():
+        send_coef(1, (gx + 1, gy)).wait_recv()
+
+    @pl.when(gx == GX - 1)
+    def _():
+        coef_halo[1] = jnp.zeros((RHS, SPAN), BF)
+
     for side in range(2):
         for pair in range(LEAVES // 2):
             expand(
@@ -433,6 +470,15 @@
 
     for halo in halos:
         halo.wait_send()
+
+    @pl.when(gx > 0)
+    def _():
+        send_coef(1, (gx - 1, gy)).wait_send()
+
+    @pl.when(gx < GX - 1)
+    def _():
+        send_coef(0, (gx + 1, gy)).wait_send()
+
     wait_all(gather_send.at[0], part_buf, GX - 1)
     wait_all(gather_send.at[1], root_buf, GY - 1)
     wait_all(gather_send.at[2], sum_buf, GY - 1)
@@ -505,6 +551,7 @@
             pltpu.SemaphoreType.DMA((4,)),
             pltpu.SemaphoreType.DMA((3,)),
             pltpu.SemaphoreType.DMA((3,)),
+            pltpu.SemaphoreType.DMA((GX,)),
         ],
         compiler_params=pltpu.CompilerParams(
             collective_id=0, has_side_effects=True, vmem_limit_bytes=32 * 2**20

time: 27.5 us -> 26.9 us (0.978)
  the two profiles are of different devices: /device:TPU:1 before, /device:TPU:6 now
where the time goes in v4:
time: 26.9 us; the launch traced here: 26.8 us
  Pallas kernels  25.5 us (95%)
  between operations  0.66 us (2%)
  local copies, waits for them, and re-layouts  0.63 us (2%)
    pallas_call x1, Pallas kernels, per_device(): pl.pallas_call(kernel, out_shape=jax.ShapeDtypeStruct((RHS, SPAN), BF), i...  25.5 us
    unnamed x1, local copies, waits for them, and re-layouts  0.63 us

profile of v4, /device:TPU:6, one launch (start us, length us, event | category | flops | bytes accessed | tf_op | source)
XLA Modules:
  0.0 26.8 jit_solution(10843062662368415119)
XLA Ops:
  0.7 25.5 %h2_product.1 = bf16[16,2048]{1,0:T(8,128)(2,1)S(1)} custom-call(bf16[16,2048]{1,0:T(8,128)(2,1)} %points.1, bf16[64,2048]{1,0:T(8,128)(2,1)} %col.1, bf16[32,64,64]{2,1,0:T(8,128)(2,1)} %up.1, bf16[1,64,64]{2,1,0:T(8,128)(2,1)} %plane_up.1, bf16[1,16,64,64]{3,2,1,0:T(8,128)(2,1)} %plane_coupling.1, bf16[32,64,256]{2,1,0:T(8,128)(2,1)} %near_blocks.1, ...), custom_call_target="tpu_custom_call" | custom-call | tf_op jit(solution)/shard_map/h2_product/pallas_call | solution.py:508
  26.1 0.6 %copy.21 = bf16[16,2048]{1,0:T(8,128)(2,1)} copy(bf16[16,2048]{1,0:T(8,128)(2,1)S(1)} %h2_product.1) | data formatting | bytes 131072

commit v5 on v4

--- a/solution.py
+++ b/solution.py
@@ -29,6 +29,12 @@
 
 def dot_nn(a, b):
     return lax.dot_general(a, b, (((1,), (0,)), ((), ())), preferred_element_type=F32)
+
+
+def place_of(gy):
+    x, y = gy >> 3, gy & 7
+    turned = jnp.where(y < 4, y, 11 - y)
+    return ((turned + x) << 5) + gy
 
 
 def kernel(
@@ -92,6 +98,7 @@
     gather_send,
     gather_recv,
     part_recv,
+    ready,
 ):
     gx = lax.axis_index("gx")
     gy = lax.axis_index("gy")
@@ -150,14 +157,24 @@
         )
         return carry
 
-    def greet_gy(i, carry):
-        pl.semaphore_signal(
-            barrier, inc=1, device_id=(gx, (gy + i) & (GY - 1)), device_id_type=MESH
-        )
+    my_place = place_of(gy)
+
+    def greet_gy(i, before):
+        @pl.when(place_of(i) > my_place)
+        def _():
+            pl.semaphore_signal(barrier, inc=1, device_id=(gx, i), device_id_type=MESH)
+
+        return before + jnp.where(place_of(i) < my_place, 1, 0)
+
+    def greet_gy_back(i, carry):
+        @pl.when(place_of(i) < my_place)
+        def _():
+            pl.semaphore_signal(ready, inc=1, device_id=(gx, i), device_id_type=MESH)
+
         return carry
 
     lax.fori_loop(gx + 1, GX, greet_gx, 0)
-    lax.fori_loop(1, GY, greet_gy, 0)
+    before = lax.fori_loop(0, GY, greet_gy, 0)
 
     lane = lax.broadcasted_iota(jnp.int32, (RHS, 128), 1)
     low = lane < RANK
@@ -205,7 +222,9 @@
     part_buf[gx] = jnp.concatenate([part, part], axis=1).astype(BF)
     root_buf[gy] = jnp.concatenate([root, root], axis=1).astype(BF)
 
-    pl.semaphore_wait(barrier, gx + GY - 1)
+    @pl.when(gx + before > 0)
+    def _():
+        pl.semaphore_wait(barrier, gx + before)
 
     def send_part(peer, carry):
         pltpu.make_async_remote_copy(
@@ -257,33 +276,12 @@
         pltpu.make_async_copy(held, held, sem).wait()
 
     lax.fori_loop(0, gx, send_part, 0)
-    next_gy = (gx, (gy + 1) & (GY - 1))
-    last_gy = (gx, (gy - 1) & (GY - 1))
-    half = BORDER * RANK
-    halos = []
-    for place, (src, dst, device) in enumerate(
-        (
-            (points_v.at[:, pl.ds(half, half)], points_halo.at[0], next_gy),
-            (points_v.at[:, pl.ds(0, half)], points_halo.at[1], last_gy),
-        )
-    ):
-        halos.append(
-            pltpu.make_async_remote_copy(
-                src_ref=src,
-                dst_ref=dst,
-                send_sem=halo_send.at[place],
-                recv_sem=halo_recv.at[place],
-                device_id=device,
-                device_id_type=MESH,
-            )
-        )
-        halos[-1].start()
+    lax.fori_loop(0, GY, greet_gy_back, 0)
 
     @pl.when(gx > 0)
     def _():
         send_coef(1, (gx - 1, gy)).start()
 
-    spread_gy(root_buf, 1)
 
     load_pc.wait()
     for pair in range(GX // 2):
@@ -315,6 +313,33 @@
     window = 2 * LEAVES
     near_left[window] = jnp.zeros((RHS, 128), BF)
     near_right[window] = jnp.zeros((RHS, 128), BF)
+
+    @pl.when(before < GY - 1)
+    def _():
+        pl.semaphore_wait(ready, GY - 1 - before)
+
+    spread_gy(root_buf, 1)
+    next_gy = (gx, (gy + 1) & (GY - 1))
+    last_gy = (gx, (gy - 1) & (GY - 1))
+    half = BORDER * RANK
+    halos = []
+    for place, (src, dst, device) in enumerate(
+        (
+            (points_v.at[:, pl.ds(half, half)], points_halo.at[0], next_gy),
+            (points_v.at[:, pl.ds(0, half)], points_halo.at[1], last_gy),
+        )
+    ):
+        halos.append(
+            pltpu.make_async_remote_copy(
+                src_ref=src,
+                dst_ref=dst,
+                send_sem=halo_send.at[place],
+                recv_sem=halo_recv.at[place],
+                device_id=device,
+                device_id_type=MESH,
+            )
+        )
+        halos[-1].start()
 
     @pl.when(gx < GX - 1)
     def _():
@@ -552,6 +577,7 @@
             pltpu.SemaphoreType.DMA((3,)),
             pltpu.SemaphoreType.DMA((3,)),
             pltpu.SemaphoreType.DMA((GX,)),
+            pltpu.SemaphoreType.REGULAR,
         ],
         compiler_params=pltpu.CompilerParams(
             collective_id=0, has_side_effects=True, vmem_limit_bytes=32 * 2**20

time: 26.9 us -> 26.7 us (level)
  the two profiles are of different devices: /device:TPU:6 before, /device:TPU:1 now
where the time goes in v5:
time: 26.7 us; the launch traced here: 26.4 us
  Pallas kernels  25.1 us (94%)
  between operations  0.66 us (2%)
  local copies, waits for them, and re-layouts  0.63 us (2%)
    pallas_call x1, Pallas kernels, per_device(): pl.pallas_call(kernel, out_shape=jax.ShapeDtypeStruct((RHS, SPAN), BF), i...  25.1 us
    unnamed x1, local copies, waits for them, and re-layouts  0.63 us

profile of v5, /device:TPU:1, one launch (start us, length us, event | category | flops | bytes accessed | tf_op | source)
XLA Modules:
  0.0 26.4 jit_solution(1777627402626688084)
XLA Ops:
  0.7 25.1 %h2_product.1 = bf16[16,2048]{1,0:T(8,128)(2,1)S(1)} custom-call(bf16[16,2048]{1,0:T(8,128)(2,1)} %points.1, bf16[64,2048]{1,0:T(8,128)(2,1)} %col.1, bf16[32,64,64]{2,1,0:T(8,128)(2,1)} %up.1, bf16[1,64,64]{2,1,0:T(8,128)(2,1)} %plane_up.1, bf16[1,16,64,64]{3,2,1,0:T(8,128)(2,1)} %plane_coupling.1, bf16[32,64,256]{2,1,0:T(8,128)(2,1)} %near_blocks.1, ...), custom_call_target="tpu_custom_call" | custom-call | tf_op jit(solution)/shard_map/h2_product/pallas_call | solution.py:533
  25.8 0.6 %copy.21 = bf16[16,2048]{1,0:T(8,128)(2,1)} copy(bf16[16,2048]{1,0:T(8,128)(2,1)S(1)} %h2_product.1) | data formatting | bytes 131072

commit v6 on v5

--- a/solution.py
+++ b/solution.py
@@ -33,7 +33,7 @@
 
 def place_of(gy):
     x, y = gy >> 3, gy & 7
-    turned = jnp.where(y < 4, y, 11 - y)
+    turned = (y if y < 4 else 11 - y) if isinstance(y, int) else jnp.where(y < 4, y, 11 - y)
     return ((turned + x) << 5) + gy
 
 
@@ -174,7 +174,9 @@
         return carry
 
     lax.fori_loop(gx + 1, GX, greet_gx, 0)
-    before = lax.fori_loop(0, GY, greet_gy, 0)
+    before = 0
+    for peer in range(GY):
+        before = greet_gy(peer, before)
 
     lane = lax.broadcasted_iota(jnp.int32, (RHS, 128), 1)
     low = lane < RANK
@@ -276,7 +278,8 @@
         pltpu.make_async_copy(held, held, sem).wait()
 
     lax.fori_loop(0, gx, send_part, 0)
-    lax.fori_loop(0, GY, greet_gy_back, 0)
+    for peer in range(GY):
+        greet_gy_back(peer, 0)
 
     @pl.when(gx > 0)
     def _():

time: 26.7 us -> 26.6 us (level)
  no operation moved by 1% of the time
where the time goes in v6:
time: 26.6 us; the launch traced here: 26.2 us
  Pallas kernels  24.9 us (94%)
  between operations  0.66 us (2%)
  local copies, waits for them, and re-layouts  0.63 us (2%)
    pallas_call x1, Pallas kernels, per_device(): pl.pallas_call(kernel, out_shape=jax.ShapeDtypeStruct((RHS, SPAN), BF), i...  24.9 us
    unnamed x1, local copies, waits for them, and re-layouts  0.63 us

profile of v6, /device:TPU:1, one launch (start us, length us, event | category | flops | bytes accessed | tf_op | source)
XLA Modules:
  0.0 26.2 jit_solution(337439801270933954)
XLA Ops:
  0.7 24.9 %h2_product.1 = bf16[16,2048]{1,0:T(8,128)(2,1)S(1)} custom-call(bf16[16,2048]{1,0:T(8,128)(2,1)} %points.1, bf16[64,2048]{1,0:T(8,128)(2,1)} %col.1, bf16[32,64,64]{2,1,0:T(8,128)(2,1)} %up.1, bf16[1,64,64]{2,1,0:T(8,128)(2,1)} %plane_up.1, bf16[1,16,64,64]{3,2,1,0:T(8,128)(2,1)} %plane_coupling.1, bf16[32,64,256]{2,1,0:T(8,128)(2,1)} %near_blocks.1, ...), custom_call_target="tpu_custom_call" | custom-call | tf_op jit(solution)/shard_map/h2_product/pallas_call | solution.py:536
  25.5 0.6 %copy.21 = bf16[16,2048]{1,0:T(8,128)(2,1)} copy(bf16[16,2048]{1,0:T(8,128)(2,1)S(1)} %h2_product.1) | data formatting | bytes 131072
